TPU v7x, 256 devices: a whole 4x4x8 slice. The times are simulated.
256 devices in a mesh: gz: 64 (over x, z, core), gy: 4 (over y).
Axes of the slice: x: 4, y: 4, z: 8, core: 2. Of those that a mesh axis runs over, the one named last changes fastest.
Arguments:
- velocity: float32 [3, 128, 8, 128], P(None, 'gz', 'gy'), may hold values from -6 to 6
- slip: float32 [3, 131072], P(None, ('gz', 'gy')), may hold values from -6 to 6
- rate: float32 [131072], P(('gz', 'gy')), may hold values from 0.5 to 4
- owner: int32 [131072, 1], P(('gz', 'gy')), may hold values from 0 to 63; in each aligned block of 512 rows (0 to 511, 512 to 1023, ...) at most 16 rows name the same one
- cell: int32 [131072], P(('gz', 'gy')), may hold values from 0 to 511
- count: int32 [256], P(('gz', 'gy')), may hold values from 256 to 512
- w_in: bfloat16 [12, 1024], replicated, may hold values from -1.75 to 1.75
- b_in: float32 [1024], replicated, may hold values from -3 to 3
- w_mid: bfloat16 [1024, 1024], replicated, may hold values from -0.1875 to 0.1875
- b_mid: float32 [1024], replicated, may hold values from -3 to 3
- w_out: bfloat16 [1024, 6], replicated, may hold values from -0.1875 to 0.1875
- tau_bar: bfloat16 [6, 128, 8, 128], P(None, 'gz', 'gy'), may hold values from -1.5 to 1.5
Outputs:
- stress: float32 [6, 128, 8, 128], P(None, 'gz', 'gy')
- velocity_bar: float32 [3, 128, 8, 128], P(None, 'gz', 'gy')
- slip_bar: float32 [3, 131072], P(None, ('gz', 'gy'))
- rate_bar: float32 [131072], P(('gz', 'gy'))
- grad_w_in: float32 [12, 1024], replicated
- grad_b_in: float32 [1024], replicated
- grad_w_mid: float32 [1024, 1024], replicated
- grad_b_mid: float32 [1024], replicated
- grad_w_out: float32 [1024, 6], replicated
Inputs may be any that keep to these rules, and one draw needn't show every extreme that they name: Each particle's cell lies in the slab owner names, in the y-range of the particle's own device index along gy. Among the 512 slots of one device, at most 16 name the same slab, and that many do for some slab. The cell is flattened in the order z, y, x of the owner's block. The first count slots of a device are live, the others empty.
All inputs are finite; a program needn't handle non-finite values.
Results may differ from a plain program's by a relative error of at most 0.007.
Values sent between devices are 32-bit elements; how exact they have to be, the bound alone decides.
A program may use at most 64 MiB of HBM per device.

v0:
```python
import jax
import jax.numpy as jnp
from jax import lax
from jax.sharding import PartitionSpec as P


def with_halo(cells, sides, width):
    for axis, dim in sides:
        count = lax.axis_size(axis)
        head = lax.slice_in_dim(cells, 0, width, axis=dim)
        tail = lax.slice_in_dim(cells, cells.shape[dim] - width, cells.shape[dim], axis=dim)
        cells = jnp.concatenate(
            [
                lax.ppermute(tail, axis, [(i, (i + 1) % count) for i in range(count)]),
                cells,
                lax.ppermute(head, axis, [((i + 1) % count, i) for i in range(count)]),
            ],
            axis=dim,
        )
    return cells


def dsilu(value):
    sig = jax.nn.sigmoid(value)
    return sig * (1.0 + value * (1.0 - sig))


def deposit(forces, cell_row, ncells):
    block = min(512, ncells)
    count_blocks = ncells // block

    def deposit_one_block(index):
        start = index * block
        onehot = (
            cell_row[0][:, None] == start + jnp.arange(block, dtype=jnp.int32)[None, :]
        ).astype(jnp.float32)
        return jnp.dot(
            forces, onehot, precision=lax.Precision.HIGHEST, preferred_element_type=jnp.float32
        )

    pieces = lax.map(deposit_one_block, jnp.arange(count_blocks, dtype=jnp.int32))
    return pieces.transpose(1, 0, 2).reshape(forces.shape[0], ncells)


def collect(values, cell_row, ncells):
    block = min(512, ncells)
    count_blocks = ncells // block

    def collect_one_block(index, total):
        start = index * block
        onehot = (
            start + jnp.arange(block, dtype=jnp.int32)[:, None] == cell_row[0][None, :]
        ).astype(jnp.float32)
        return total + jnp.dot(
            values, onehot, precision=lax.Precision.HIGHEST, preferred_element_type=jnp.float32
        )

    init = jnp.zeros((values.shape[0], cell_row.shape[1]), jnp.float32)
    return lax.fori_loop(0, count_blocks, collect_one_block, init)


def roll_diff(field):
    return (jnp.roll(field, -1, 3) - jnp.roll(field, 1, 3)) * 0.5


def shards(velocity, slip, rate, owner, cell, count, w_in, b_in, w_mid, b_mid, w_out, tau_bar):
    nparts = slip.shape[1]
    slabs = lax.axis_size("gz")
    capacity = 2 * nparts // slabs
    width_all = slabs * capacity
    ncz, ncy, ncx = (velocity.shape[1], velocity.shape[2], velocity.shape[3])
    ncells = ncz * ncy * ncx
    padded = with_halo(velocity, (("gz", 1), ("gy", 2)), 1)
    core = padded[:, 1:-1, 1:-1]
    along_z = (padded[:, 2:, 1:-1] - padded[:, :-2, 1:-1]) * 0.5
    along_y = (padded[:, 1:-1, 2:] - padded[:, 1:-1, :-2]) * 0.5
    grads = jnp.stack([along_z, along_y, roll_diff(core)], 1).reshape(9, ncells)
    live = jnp.arange(nparts, dtype=jnp.int32) < count[0]
    force = jnp.where(live[None, :], rate[None, :] * slip, 0.0)
    owners = owner[:, 0]
    member = (owners[:, None] == jnp.arange(slabs, dtype=jnp.int32)[None, :]).astype(jnp.int32)
    before = jnp.cumsum(member, 0) - member
    position = jnp.sum(before * member, 1)
    slot = owners * capacity + position
    send_force = jnp.zeros((3, width_all), jnp.float32).at[:, slot].set(force)
    send_cell = jnp.full((1, width_all), -1, jnp.int32).at[0, slot].set(jnp.where(live, cell, -1))
    recv_force, recv_cell = (
        lax.all_to_all(send_force, "gz", split_axis=1, concat_axis=1, tiled=True),
        lax.all_to_all(send_cell, "gz", split_axis=1, concat_axis=1, tiled=True),
    )
    source = deposit(recv_force, recv_cell, ncells)
    feats = jnp.concatenate([grads, source], 0).astype(jnp.bfloat16)
    tbar = tau_bar.reshape(tau_bar.shape[0], ncells)
    pre1 = jnp.einsum("fh,fc->hc", w_in, feats, preferred_element_type=jnp.float32) + b_in[:, None]
    hidden_one = jax.nn.silu(pre1).astype(jnp.bfloat16)
    pre2 = (
        jnp.einsum("gh,gc->hc", w_mid, hidden_one, preferred_element_type=jnp.float32)
        + b_mid[:, None]
    )
    hidden_two = jax.nn.silu(pre2).astype(jnp.bfloat16)
    stress = jnp.einsum("ho,hc->oc", w_out, hidden_two, preferred_element_type=jnp.float32)
    grad_w_out = jnp.einsum("hc,oc->ho", hidden_two, tbar, preferred_element_type=jnp.float32)
    back_two = jnp.einsum("ho,oc->hc", w_out, tbar, preferred_element_type=jnp.float32)
    delta_two = (back_two * dsilu(pre2)).astype(jnp.bfloat16)
    grad_w_mid = jnp.einsum("gc,hc->gh", hidden_one, delta_two, preferred_element_type=jnp.float32)
    grad_b_mid = jnp.sum(delta_two.astype(jnp.float32), 1)
    back_one = jnp.einsum("gh,hc->gc", w_mid, delta_two, preferred_element_type=jnp.float32)
    delta_one = (back_one * dsilu(pre1)).astype(jnp.bfloat16)
    grad_w_in = jnp.einsum("fc,hc->fh", feats, delta_one, preferred_element_type=jnp.float32)
    grad_b_in = jnp.sum(delta_one.astype(jnp.float32), 1)
    grad_w_in, grad_b_in, grad_w_mid, grad_b_mid, grad_w_out = lax.psum(
        (grad_w_in, grad_b_in, grad_w_mid, grad_b_mid, grad_w_out), ("gz", "gy")
    )
    feats_bar = jnp.einsum("fh,hc->fc", w_in, delta_one, preferred_element_type=jnp.float32)
    grads_bar = feats_bar[:9].reshape(3, 3, ncz, ncy, ncx)
    joint = with_halo(grads_bar.reshape(9, ncz, ncy, ncx), (("gz", 1), ("gy", 2)), 1)
    joint = joint.reshape(3, 3, ncz + 2, ncy + 2, ncx)
    term_z = (joint[:, 0, 2:, 1:-1] - joint[:, 0, :-2, 1:-1]) * 0.5
    term_y = (joint[:, 1, 1:-1, 2:] - joint[:, 1, 1:-1, :-2]) * 0.5
    term_x = roll_diff(joint[:, 2, 1:-1, 1:-1])
    velocity_bar = -(term_z + term_y + term_x)
    source_bar = feats_bar[9:12]
    per_slot = collect(source_bar, recv_cell, ncells)
    returned = lax.all_to_all(per_slot, "gz", split_axis=1, concat_axis=1, tiled=True)
    at_particle = returned[:, slot]
    slip_bar = jnp.where(live[None, :], rate[None, :] * at_particle, 0.0)
    rate_bar = jnp.where(live, jnp.sum(slip * at_particle, 0), 0.0)
    return (
        stress.reshape(stress.shape[0], ncz, ncy, ncx),
        velocity_bar,
        slip_bar,
        rate_bar,
        grad_w_in,
        grad_b_in,
        grad_w_mid,
        grad_b_mid,
        grad_w_out,
    )


def solution(mesh):
    return jax.shard_map(
        shards,
        mesh=mesh,
        in_specs=(
            P(None, "gz", "gy", None),
            P(None, ("gz", "gy")),
            P(("gz", "gy")),
            P(("gz", "gy"), None),
            P(("gz", "gy")),
            P(("gz", "gy")),
            P(),
            P(),
            P(),
            P(),
            P(),
            P(None, "gz", "gy", None),
        ),
        out_specs=(
            P(None, "gz", "gy", None),
            P(None, "gz", "gy", None),
            P(None, ("gz", "gy")),
            P(("gz", "gy")),
            P(),
            P(),
            P(),
            P(),
            P(),
        ),
        check_vma=False,
    )
```

profile of v0, /device:TPU:1, one launch (start us, length us, event | category | flops | bytes accessed | tf_op | source)
XLA Modules:
  0.0 600.4 jit_solution(1143076900839981350)
XLA Ops:
  7.2 0.9 fusion.62
  8.0 3.2 collective-permute-start
  11.9 0.7 fusion.28
  12.7 1.2 reduce-window.6
  14.1 0.8 fusion.27
  14.9 0.7 compare_select_fusion
  15.6 0.7 broadcast_select_fusion.1
  16.3 2.4 scatter_custom_fusion.1
  18.8 0.7 all_to_all.25
  19.4 12.6 %all-to-all-start.1 = ((s32[1,64,16]{2,0,1:T(1,128)}), s32[1,64,16]{2,0,1:T(1,128)S(1)}, u32[]{:S(2)}, u32[]{:S(2)}) async-start(s32[1,64,16]{2,0,1:T(1,128)} %bitcast.14), calls=%async_computation.1 | async-start | bytes 65536 | tf_op jit(solution)/shard_map/all_to_all | solution.py:89
  32.1 0.8 slice_bitcast_fusion.5
  32.9 0.8 fusion.63
  33.8 0.7 multiply_select_fusion
  35.0 0.8 fusion.47
  35.8 2.8 collective-permute-start.2
  38.7 0.8 copy.88
  39.5 0.7 reshape.131
  40.4 1.9 scatter_custom_fusion
  42.3 1.1 copy.79
  43.4 10.6 %all-to-all-start = ((f32[3,64,16]{2,0,1:T(4,128)}), f32[3,64,16]{2,0,1:T(4,128)S(1)}, u32[]{:S(2)}, u32[]{:S(2)}) async-start(f32[3,64,16]{2,0,1:T(4,128)} %copy.79), calls=%async_computation | async-start | bytes 262144 | tf_op jit(solution)/shard_map/all_to_all | solution.py:88
  54.2 0.5 broadcast.94
  54.7 0.7 reduce.5
  55.7 8.7 %all-to-all-done = f32[3,64,16]{2,0,1:T(4,128)S(1)} async-done(((f32[3,64,16]{2,0,1:T(4,128)}), f32[3,64,16]{2,0,1:T(4,128)S(1)}, u32[]{:S(2)}, u32[]{:S(2)}) %all-to-all-start) | async-done | bytes 12320 | tf_op jit(solution)/shard_map/all_to_all | solution.py:88
  64.5 0.8 fusion.17
  65.8 1.6 fusion.4
  67.8 0.9 fusion.64
  68.7 1.6 convert_reduce_fusion
  70.3 2.4 convert_reduce_fusion.1
  73.0 0.9 fusion.29
  73.9 3.3 fusion.53
  77.4 1.4 collective-permute-start.4
  78.8 0.8 fusion.16
  79.5 0.6 reshape.130
  80.3 0.7 copy.86
  81.0 8.2 %all-to-all-start.2 = ((f32[3,64,16]{2,0,1:T(4,128)}), f32[3,64,16]{2,0,1:T(4,128)S(1)}, u32[]{:S(2)}, u32[]{:S(2)}) async-start(f32[3,64,16]{2,0,1:T(4,128)} %copy.86), calls=%async_computation.2 | async-start | bytes 262144 | tf_op jit(solution)/shard_map/all_to_all | solution.py:124
  89.7 2.7 collective-permute-start.7
  92.4 7.3 %all-to-all-done.2 = f32[3,64,16]{2,0,1:T(4,128)S(1)} async-done(((f32[3,64,16]{2,0,1:T(4,128)}), f32[3,64,16]{2,0,1:T(4,128)S(1)}, u32[]{:S(2)}, u32[]{:S(2)}) %all-to-all-start.2) | async-done | bytes 12320 | tf_op jit(solution)/shard_map/all_to_all | solution.py:124
  100.1 1.0 gather_fusion
  101.5 0.6 broadcast_select_fusion
  102.1 0.7 copy.89
  103.0 0.7 fusion.46
  103.7 211.7 %all-reduce.7.cloned.1.call-done = (f32[12,1024]{1,0:T(8,128)}, f32[1024]{0:T(1024)}, f32[1024]{0:T(1024)}, f32[1024,6]{0,1:T(8,128)}) async-done(((f32[12,1024]{1,0:T(8,128)}, f32[1024]{0:T(1024)}, f32[1024]{0:T(1024)}, f32[1024,6]{0,1:T(8,128)}), (f32[12,1024]{1,0:T(8,128)}, f32[1024]{0:T(1024)}, f32[1024]{0:T(1024)}, f32[1024,6]{0,1:T(8,128)})) %all-reduce.7.cloned.1.call-update) | async-done | bytes 81936 | tf_op jit(solution)/shard_map/psum | solution.py:111
  315.4 269.4 %all-reduce.5.cloned.1.call-done = f32[1024,1024]{1,0:T(8,128)} async-done(((f32[1024,1024]{1,0:T(8,128)}), f32[1024,1024]{1,0:T(8,128)}) %all-reduce.5.cloned.1.call-update) | async-done | bytes 4194320 | tf_op jit(solution)/shard_map/psum | solution.py:111
  584.8 1.5 copy.111
  586.3 1.3 copy.112
  587.6 4.8 copy.113
  592.4 0.6 copy.114
  593.0 0.6 copy.115
  (70 shorter events, 4.3 us)
Async XLA Ops:
  7.2 58.6 %copy-start = (bf16[1024,1024]{1,0:T(8,128)(2,1)S(1)}, bf16[1024,1024]{1,0:T(8,128)(2,1)}, u32[]{:S(2)}) copy-start(bf16[1024,1024]{1,0:T(8,128)(2,1)} %param.20) | copy-start | bytes 6291460
  8.0 26.9 %collective-permute-start = (f32[3,1,2,128]{3,2,1,0:T(2,128)S(1)}, f32[3,1,2,128]{3,2,1,0:T(2,128)S(1)}, u32[]{:S(2)}, u32[]{:S(2)}) collective-permute-start(f32[3,1,2,128]{3,2,1,0:T(2,128)S(1)} %get-tuple-element.90), channel_id=1, source_target_pairs={{4,0},{8,4},{12,8},{16,12},{20,16},{24,20},{28,24},{32,28},{36,32}... | collective-permute-start | bytes 9224 | tf_op jit(solution)/shard_map/ppermute | solution.py:16
  11.3 23.7 %collective-permute-start.1 = (f32[3,1,2,128]{3,2,1,0:T(2,128)S(1)}, f32[3,1,2,128]{3,2,1,0:T(2,128)S(1)}, u32[]{:S(2)}, u32[]{:S(2)}) collective-permute-start(f32[3,1,2,128]{3,2,1,0:T(2,128)S(1)} %get-tuple-element.91), channel_id=1, source_target_pairs={{0,4},{4,8},{8,12},{12,16},{16,20},{20,24},{24,28},{28,32},{32,36}... | collective-permute-start | bytes 9224 | tf_op jit(solution)/shard_map/ppermute | solution.py:14
  12.6 52.6 %copy-start.1 = (bf16[12,1024]{1,0:T(8,128)(2,1)S(1)}, bf16[12,1024]{1,0:T(8,128)(2,1)}, u32[]{:S(2)}) copy-start(bf16[12,1024]{1,0:T(8,128)(2,1)} %param.18) | copy-start | bytes 73732
  19.4 23.9 %all-to-all-start.1 = ((s32[1,64,16]{2,0,1:T(1,128)}), s32[1,64,16]{2,0,1:T(1,128)S(1)}, u32[]{:S(2)}, u32[]{:S(2)}) async-start(s32[1,64,16]{2,0,1:T(1,128)} %bitcast.14), calls=%async_computation.1 | async-start | bytes 65536 | tf_op jit(solution)/shard_map/all_to_all | solution.py:89
  35.8 19.8 %collective-permute-start.2 = (f32[3,4,1,128]{3,2,1,0:T(1,128)S(1)}, f32[3,4,1,128]{3,2,1,0:T(1,128)S(1)}, u32[]{:S(2)}, u32[]{:S(2)}) collective-permute-start(f32[3,4,1,128]{3,2,1,0:T(1,128)S(1)} %get-tuple-element.82), channel_id=1, source_target_pairs={{1,0},{2,1},{3,2},{0,3},{5,4},{6,5},{7,6},{4,7},{9,8},{10,9},{11,1... | collective-permute-start | bytes 18440 | tf_op jit(solution)/shard_map/ppermute | solution.py:16
  38.6 17.0 %collective-permute-start.3 = (f32[3,4,1,128]{3,2,1,0:T(1,128)S(1)}, f32[3,4,1,128]{3,2,1,0:T(1,128)S(1)}, u32[]{:S(2)}, u32[]{:S(2)}) collective-permute-start(f32[3,4,1,128]{3,2,1,0:T(1,128)S(1)} %get-tuple-element.83), channel_id=1, source_target_pairs={{0,1},{1,2},{2,3},{3,0},{4,5},{5,6},{6,7},{7,4},{8,9},{9,10},{10,1... | collective-permute-start | bytes 18440 | tf_op jit(solution)/shard_map/ppermute | solution.py:14
  42.3 23.5 %copy-start.6 = (f32[1024]{0:T(1024)S(1)}, f32[1024]{0:T(1024)}, u32[]{:S(2)}) copy-start(f32[1024]{0:T(1024)} %param.21) | copy-start | bytes 12292
  42.3 23.5 %copy-start.7 = (f32[1024]{0:T(1024)S(1)}, f32[1024]{0:T(1024)}, u32[]{:S(2)}) copy-start(f32[1024]{0:T(1024)} %param.19) | copy-start | bytes 12292
  43.4 21.0 %all-to-all-start = ((f32[3,64,16]{2,0,1:T(4,128)}), f32[3,64,16]{2,0,1:T(4,128)S(1)}, u32[]{:S(2)}, u32[]{:S(2)}) async-start(f32[3,64,16]{2,0,1:T(4,128)} %copy.79), calls=%async_computation | async-start | bytes 262144 | tf_op jit(solution)/shard_map/all_to_all | solution.py:88
  54.0 261.4 %all-reduce.7.cloned.1.call-start = ((), (), s32[]{:S(2)}) async-start(), calls=%async_computation.4 | async-start | bytes 212992 | tf_op jit(solution)/shard_map/psum | solution.py:111
  65.8 1.6 copy-start.3
  77.3 507.5 %all-reduce.5.cloned.1.call-start = ((), (), s32[]{:S(2)}) async-start(), calls=%async_computation.3 | async-start | bytes 8388608 | tf_op jit(solution)/shard_map/psum | solution.py:111
  77.4 23.8 %copy-start.4 = (f32[512]{0:T(512)S(1)}, f32[512]{0:T(512)}, u32[]{:S(2)}) copy-start(f32[512]{0:T(512)} %param.14) | copy-start | bytes 6148
  77.4 11.8 %collective-permute-start.4 = (f32[9,1,2,128]{3,2,1,0:T(2,128)S(1)}, f32[9,1,2,128]{3,2,1,0:T(2,128)S(1)}, u32[]{:S(2)}, u32[]{:S(2)}) collective-permute-start(f32[9,1,2,128]{3,2,1,0:T(2,128)S(1)} %get-tuple-element.81), channel_id=1, source_target_pairs={{0,4},{4,8},{8,12},{12,16},{16,20},{20,24},{24,28},{28,32},{32,36}... | collective-permute-start | bytes 27656 | tf_op jit(solution)/shard_map/ppermute | solution.py:14
  80.2 9.1 %collective-permute-start.5 = (f32[9,1,2,128]{3,2,1,0:T(2,128)S(1)}, f32[9,1,2,128]{3,2,1,0:T(2,128)S(1)}, u32[]{:S(2)}, u32[]{:S(2)}) collective-permute-start(f32[9,1,2,128]{3,2,1,0:T(2,128)S(1)} %get-tuple-element.80), channel_id=1, source_target_pairs={{4,0},{8,4},{12,8},{16,12},{20,16},{24,20},{28,24},{32,28},{36,32}... | collective-permute-start | bytes 27656 | tf_op jit(solution)/shard_map/ppermute | solution.py:16
  81.0 18.7 %all-to-all-start.2 = ((f32[3,64,16]{2,0,1:T(4,128)}), f32[3,64,16]{2,0,1:T(4,128)S(1)}, u32[]{:S(2)}, u32[]{:S(2)}) async-start(f32[3,64,16]{2,0,1:T(4,128)} %copy.86), calls=%async_computation.2 | async-start | bytes 262144 | tf_op jit(solution)/shard_map/all_to_all | solution.py:124
  89.3 13.5 %collective-permute-start.6 = (f32[9,4,1,128]{3,2,1,0:T(1,128)S(1)}, f32[9,4,1,128]{3,2,1,0:T(1,128)S(1)}, u32[]{:S(2)}, u32[]{:S(2)}) collective-permute-start(f32[9,4,1,128]{3,2,1,0:T(1,128)S(1)} %get-tuple-element.78), channel_id=1, source_target_pairs={{0,1},{1,2},{2,3},{3,0},{4,5},{5,6},{6,7},{7,4},{8,9},{9,10},{10,1... | collective-permute-start | bytes 55304 | tf_op jit(solution)/shard_map/ppermute | solution.py:14
  89.7 13.1 %collective-permute-start.7 = (f32[9,4,1,128]{3,2,1,0:T(1,128)S(1)}, f32[9,4,1,128]{3,2,1,0:T(1,128)S(1)}, u32[]{:S(2)}, u32[]{:S(2)}) collective-permute-start(f32[9,4,1,128]{3,2,1,0:T(1,128)S(1)} %get-tuple-element.79), channel_id=1, source_target_pairs={{1,0},{2,1},{3,2},{0,3},{5,4},{6,5},{7,6},{4,7},{9,8},{10,9},{11,1... | collective-permute-start | bytes 55304 | tf_op jit(solution)/shard_map/ppermute | solution.py:16
  587.6 4.8 copy-start.5
  587.6 5.4 copy-start.2
Sparse Core Ops, SparseCore 0:
  77.4 237.8 all-reduce.6
  321.4 263.3 all-reduce.4
where the time goes:
time: 602 us; the launch traced here: 600 us
  waiting for transfers between devices  497 us (83%)
  starting transfers between devices  42.3 us (7%)
  local copies, waits for them, and re-layouts  24.4 us (4%)
  between operations  15 us (2%)
  matrix products  13.5 us (2%)
  other arithmetic  8.1 us (1%)
    psum x2, waiting for transfers between devices, shards(): lax.psum((grad_w_in, grad_b_in, grad_w_mid, grad_b_mid, grad_w_out), ('gz...  481 us
    all_to_all x1, starting transfers between devices, shards(): lax.all_to_all(send_cell, 'gz', split_axis=1, concat_axis=1, tiled=True)  12.6 us
  transfers between devices with their start and end apart: 13, of which 4 were waited for; matrix products, arithmetic and copies ran while one was open for 4% of the time, Pallas kernels for 0%

commit v1 on v0

v1 whole, which is shorter than its diff:
```python
import jax
import jax.numpy as jnp
from jax import lax
from jax.experimental import pallas as pl
from jax.experimental.pallas import tpu as pltpu
from jax.sharding import PartitionSpec as P

F32, BF16, I32 = jnp.float32, jnp.bfloat16, jnp.int32
NX_, NZ_, NC_, NY_ = 4, 8, 2, 4
HID, CELLS, SLOTS, CAP = 1024, 512, 512, 16
BLK = 256
NBLK = HID // BLK

(
    G_P1,
    G_P2,
    G_H1,
    G_H2,
    G_RZ,
    G_RX,
    G_SC,
    G_S1,
    G_S2,
    G_S3,
    G_S5,
    G_S6,
    G_S7,
    G_BIG,
) = range(14)
B_CORE, B_R1, B_R2, B_RZ, B_GZ, B_G2, B_G1, B_FO, B_FR = (G_BIG + NBLK * i for i in range(9))
N_SEMS = G_BIG + NBLK * 9


def nn(a, b):
    return lax.dot_general(a, b, (((1,), (0,)), ((), ())), preferred_element_type=F32)


def nt(a, b):
    return lax.dot_general(a, b, (((1,), (1,)), ((), ())), preferred_element_type=F32)


def tn(a, b):
    return lax.dot_general(a, b, (((0,), (0,)), ((), ())), preferred_element_type=F32)


def three(value):
    high = value.astype(BF16).astype(F32)
    rest = value - high
    middle = rest.astype(BF16).astype(F32)
    return high, middle, rest - middle


def iota(shape, axis):
    return lax.broadcasted_iota(I32, shape, axis)


def body(
    pk,
    cnt,
    w_in,
    b_in,
    w_mid_any,
    b_mid,
    w_out,
    out,
    sm_out,
    po,
    w_mid,
    w_in16,
    w_out16,
    v4,
    hz,
    hy,
    feats,
    m_send,
    r1,
    t1,
    r2,
    onehot,
    fs,
    back2,
    h1,
    h1t,
    ds1,
    h2t,
    g2t,
    g1t,
    cs,
    cb,
    a1,
    b1,
    p2,
    b2,
    p3,
    b3,
    zz,
    y2,
    ssm,
    sc,
    sa,
    sb1,
    spt,
    sb2,
    sz,
    sy,
    sx,
    sxo,
    fb4,
    hz2,
    hy2,
    rts,
    u2,
    t2,
    bk,
    send,
    recv,
    local,
):
    gz, gy = lax.axis_index("gz"), lax.axis_index("gy")
    x, z, c, y = gz // 16, (gz // 2) % 8, gz % 2, gy
    xc = x * 2 + c

    def dev(px, py, pz, pc):
        return {
            "gz": (lax.rem(px, NX_) * NZ_ + lax.rem(pz, NZ_)) * NC_ + lax.rem(pc, NC_),
            "gy": lax.rem(py, NY_),
        }

    def line(gz_, gy_):
        return {"gz": lax.rem(gz_, NX_ * NZ_ * NC_), "gy": lax.rem(gy_, NY_)}

    def start(group, src, dst, where):
        pltpu.make_async_remote_copy(
            src_ref=src,
            dst_ref=dst,
            send_sem=send.at[group],
            recv_sem=recv.at[group],
            device_id=where,
            device_id_type=pl.DeviceIdType.MESH,
        ).start()

    def arrived(group, whole):
        pltpu.make_async_copy(whole, whole, recv.at[group]).wait()

    def left(group, whole):
        pltpu.make_async_copy(whole, whole, send.at[group]).wait()

    load_w = pltpu.make_async_copy(w_mid_any, w_mid, local.at[0])
    load_w.start()

    sibling = dev(x, y, z, c + 1)
    partners = [dev(x + k // 2, y, z, c + k % 2) for k in range(1, 8)]
    partners += [dev(x, y + k, z, c) for k in range(1, 4)]
    partners += [dev(x, y, z + k, c) for k in range(1, 8)]
    partners += [line(gz + 63 + 2 * c, gy)]
    barrier = pltpu.get_barrier_semaphore()
    for who in partners:
        pl.semaphore_signal(barrier, inc=1, device_id=who, device_id_type=pl.DeviceIdType.MESH)

    for k in range(4):
        v4[k] = pk[0:8, 128 * k : 128 * k + 128]
    lane = iota((1, SLOTS), 1)
    live = lane < cnt[0]
    owner = pk[14:15, :].astype(I32)
    row = (owner >> 4) * 16 + (owner & 1) * 8 + ((owner >> 1) & 7)
    member = jnp.where(iota((64, SLOTS), 0) == row, 1.0, 0.0)
    member16 = member.astype(BF16)
    earlier = jnp.where(iota((SLOTS, SLOTS), 0) < iota((SLOTS, SLOTS), 1), 1.0, 0.0).astype(BF16)
    place = jnp.sum(nn(member16, earlier) * member, axis=0, keepdims=True).astype(I32)
    force = jnp.where(live, pk[6:7, :] * pk[3:6, :], 0.0)
    four = jnp.concatenate([force, pk[7:8, :]], 0)
    sub = iota((128, SLOTS), 0)
    mine = (sub // 4) == place
    wide = jnp.where(mine, jnp.concatenate([four] * 32, 0), 0.0)
    packed = nt(member16, jnp.concatenate(three(wide), 0).astype(BF16))
    packed = packed[:, 0:128] + packed[:, 128:256] + packed[:, 256:384]
    m_send[...] = packed.reshape(8, 8, 128)

    pl.semaphore_wait(barrier, len(partners))

    for k in range(1, 8):
        px, pc = lax.rem(x + k // 2, NX_), lax.rem(c + k % 2, NC_)
        start(G_P1, m_send.at[px * 2 + pc], r1.at[xc], dev(px, y, z, pc))

    def halo(group, src, to_z, to_y):
        start(group, src.at[pl.ds(2, 2)], to_z.at[0], line(gz + 1, gy))
        start(group, src.at[pl.ds(0, 2)], to_z.at[1], line(gz + 63, gy))
        start(group, src.at[1], to_y.at[0, 0], line(gz, gy + 1))
        start(group, src.at[3], to_y.at[0, 1], line(gz, gy + 1))
        start(group, src.at[0], to_y.at[1, 0], line(gz, gy + 3))
        start(group, src.at[2], to_y.at[1, 1], line(gz, gy + 3))

    halo(G_H1, v4, hz, hy)

    w_in16[...] = jnp.zeros_like(w_in16)
    w_in16[0:12, :] = w_in[...].astype(F32)
    w_out16[...] = jnp.zeros_like(w_out16)
    w_out16[0:6, :] = w_out[...].astype(F32)
    tau = jnp.concatenate([pk[8:14, :], jnp.zeros((10, CELLS), F32)], 0)
    tau16 = tau.astype(BF16)
    tau_one = jnp.where(iota((16, CELLS), 0) == 6, 1.0, tau).astype(BF16)

    def back_two(q, carry):
        cols = pl.ds(pl.multiple_of(q * BLK, BLK), BLK)
        back2[:, cols] = tn(tau16, w_out16[:, cols].astype(BF16))
        return carry

    lax.fori_loop(0, NBLK, back_two, 0)

    r1[xc] = m_send[xc]
    arrived(G_P1, r1.at[pl.ds(0, 7)])
    for k in range(8):
        t1[k] = r1[:, k, :]
    for k in range(1, 8):
        pz = lax.rem(z + k, NZ_)
        start(G_P2, t1.at[pz], r2.at[z], dev(x, y, pz, c))
    r2[z] = t1[z]

    def difference(tiles, from_z, from_y, k):
        kz, ky = k // 2, k % 2
        dz = (tiles[2 + ky] - from_z[0, ky]) if kz == 0 else (from_z[1, ky] - tiles[ky])
        dy = (tiles[2 * kz + 1] - from_y[0, kz]) if ky == 0 else (from_y[1, kz] - tiles[2 * kz])
        return dz * 0.5, dy * 0.5

    def along_x(value):
        return (pltpu.roll(value, 127, 1) - pltpu.roll(value, 1, 1)) * 0.5

    arrived(G_H1, r1)
    feats[...] = jnp.where(iota((16, CELLS), 0) == 12, 1.0, 0.0)
    for k in range(4):
        dz, dy = difference(v4, hz, hy, k)
        for a, d in enumerate((dz, dy, along_x(v4[k]))):
            for i in range(3):
                feats[3 * i + a : 3 * i + a + 1, 128 * k : 128 * k + 128] = d[i : i + 1]

    arrived(G_P2, r2.at[pl.ds(0, 7)])
    got = r2[...].reshape(64, 128)
    cell_of = iota((64, CELLS), 1).astype(F32)
    group_of = iota((64, 128), 1) // 4
    parts = three(got)
    for s in range(CAP):
        rows = slice(64 * s, 64 * s + 64)
        onehot[rows, :] = jnp.where(got[:, 4 * s + 3 : 4 * s + 4] == cell_of, 1.0, 0.0).astype(BF16)
        for j, part in enumerate(parts):
            fs[rows, 128 * j : 128 * j + 128] = jnp.where(group_of == s, part, 0.0).astype(BF16)

    def fold(wide_):
        total = wide_[0:128] + wide_[128:256] + wide_[256:384]
        total = jnp.sum(total.reshape(16, 8, total.shape[1]), axis=0)
        return total[0:3] + total[4:7]

    feats[9:12, :] = fold(tn(fs[...], onehot[...]))
    load_w.wait()

    feats16 = feats[...].astype(BF16)

    def first(q, carry):
        cols = pl.ds(pl.multiple_of(q * BLK, BLK), BLK)
        pre = tn(feats16, w_in16[:, cols].astype(BF16)) + b_in[:, cols]
        sig = jax.nn.sigmoid(pre)
        hidden = pre * sig
        h1t[:, cols] = hidden.astype(BF16)
        ds1[:, cols] = sig * (1.0 + pre * (1.0 - sig))
        h1[cols, :] = hidden.T.astype(BF16)
        return carry

    lax.fori_loop(0, NBLK, first, 0)

    def me1(p):
        return x * (1 - p) + y * p

    def me2(p):
        return y * (1 - p) + x * p

    def peer1(p, k):
        return dev(x + k * (1 - p), y + k * p, z, c)

    def peer2(p, k):
        return dev(x + k * p, y + k * (1 - p), z, c)

    def s1(q):
        p = lax.rem(q, 2)
        arrived(B_CORE + q, cb.at[q])
        a1[q] = a1[q] + cb[q]
        for k in (2, 1, 3):
            to = lax.rem(me1(p) + k, 4)
            rows = pl.ds(pl.multiple_of(to * 128, 128), 128)
            start(B_R1 + q, a1.at[q, rows], b1.at[q, k - 1], peer1(p, k))

    half = HID // 2

    def second(q, carry):
        cols = pl.ds(pl.multiple_of(q * BLK, BLK), BLK)
        pre = nn(h1t[...], w_mid[:, cols]) + b_mid[:, cols]
        sig = jax.nn.sigmoid(pre)
        hidden = (pre * sig).astype(BF16)
        h2t[:, cols] = hidden
        delta = (back2[:, cols] * (sig * (1.0 + pre * (1.0 - sig)))).astype(BF16)
        g2t[:, cols] = delta
        cs[q] = nn(h1[pl.ds(pl.multiple_of((1 - c) * half, half), half), :], delta)
        start(B_CORE + q, cs.at[q], cb.at[q], sibling)
        a1[q] = nn(h1[pl.ds(pl.multiple_of(c * half, half), half), :], delta)
        by_hidden, by_delta = nn(tau_one, hidden), nn(tau_one, delta)
        ssm[16:32, cols] = jnp.where(iota((16, BLK), 0) == 6, by_delta, by_hidden)

        @pl.when(q > 0)
        def _():
            s1(q - 1)

        return carry

    lax.fori_loop(0, NBLK, second, 0)
    s1(NBLK - 1)

    def third(q, carry):
        cols = pl.ds(pl.multiple_of(q * BLK, BLK), BLK)
        delta = (nt(g2t[...], w_mid[cols, :]) * ds1[:, cols]).astype(BF16)
        g1t[:, cols] = delta
        ssm[0:16, cols] = nn(feats16, delta)
        return carry

    lax.fori_loop(0, NBLK, third, 0)
    start(G_SC, ssm.at[pl.ds(pl.multiple_of((1 - c) * 16, 16), 16)], sc, sibling)

    bar = nt(w_in16[...].astype(BF16), g1t[...])
    for k in range(4):
        fb4[k] = bar[0:8, 128 * k : 128 * k + 128]
    halo(G_H2, fb4, hz2, hy2)
    spread = jnp.concatenate([bar[9:12], jnp.zeros((1, CELLS), F32)], 0)
    spread = jnp.concatenate([spread] * 32, 0)
    picked = nt(onehot[...], jnp.concatenate(three(spread), 0).astype(BF16))
    back = jnp.zeros((64, 128), F32)
    for s in range(CAP):
        block = picked[64 * s : 64 * s + 64]
        block = block[:, 0:128] + block[:, 128:256] + block[:, 256:384]
        back = jnp.where(group_of == s, block, back)
    rts[...] = back.reshape(8, 8, 128)
    for k in range(1, 8):
        pz = lax.rem(z + k, NZ_)
        start(G_RZ, rts.at[pz], u2.at[z], dev(x, y, pz, c))
    u2[z] = rts[z]
    po[0:6, :] = nt(w_out16[...].astype(BF16), h2t[...])[0:6]

    def s2(q):
        p = q % 2
        arrived(B_R1 + q, b1.at[q])
        own = a1[q, pl.ds(pl.multiple_of(me1(p) * 128, 128), 128), :]
        p2[q] = own + b1[q, 0] + b1[q, 1] + b1[q, 2]
        for k in (2, 1, 3):
            to = lax.rem(me2(p) + k, 4)
            start(
                B_R2 + q, p2.at[q, pl.ds(pl.multiple_of(to * 32, 32), 32)], b2.at[q, k - 1], peer2(p, k)
            )

    def s3(q):
        p = q % 2
        arrived(B_R2 + q, b2.at[q])
        own = p2[q, pl.ds(pl.multiple_of(me2(p) * 32, 32), 32), :]
        total = own + b2[q, 0] + b2[q, 1] + b2[q, 2]
        for k in range(8):
            r, cc = k // 2, k % 2
            p3[q, k] = total[8 * r : 8 * r + 8, 128 * cc : 128 * cc + 128]
        for k in (4, 3, 5, 2, 6, 1, 7):
            pz = lax.rem(z + k, NZ_)
            start(B_RZ + q, p3.at[q, pz], b3.at[q, k - 1], dev(x, y, pz, c))

    def s4(q):
        arrived(B_RZ + q, b3.at[q])
        zz[q, z] = p3[q, z] + jnp.sum(b3[q], axis=0)
        for k in (4, 3, 5, 2, 6, 1, 7):
            start(B_GZ + q, zz.at[q, z], zz.at[q, z], dev(x, y, z + k, c))

    def s5(q):
        p = q % 2
        arrived(B_GZ + q, b3.at[q])
        own = pl.multiple_of(me2(p) * 32, 32)
        for k in range(8):
            r, cc = k // 2, k % 2
            y2[q, pl.ds(own + 8 * r, 8), 128 * cc : 128 * cc + 128] = zz[q, k]
        piece = y2.at[q, pl.ds(own, 32)]
        for k in (2, 1, 3):
            start(B_G2 + q, piece, piece, peer2(p, k))

    def region(q, core, d1):
        return out.at[pl.ds(pl.multiple_of(core * half + d1 * 128, 128), 128), BLK * q : BLK * q + BLK]

    def s6(q):
        p = q % 2
        arrived(B_G2 + q, b2.at[q])
        for k in (2, 1, 3):
            start(B_G1 + q, y2.at[q], region(q, c, me1(p)), peer1(p, k))
        start(B_FO + q, y2.at[q], region(q, c, me1(p)), sibling)
        out[pl.ds(pl.multiple_of(c * half + me1(p) * 128, 128), 128), BLK * q : BLK * q + BLK] = y2[q]

    def s7(q):
        p = q % 2
        arrived(B_G1 + q, b1.at[q])
        for k in (1, 2, 3):
            where = region(q, c, lax.rem(me1(p) + k, 4))
            start(B_FR + q, where, where, sibling)

    def s8(q):
        arrived(B_FO + q, p2.at[q])
        arrived(B_FR + q, b1.at[q])

    def m1():
        arrived(G_SC, sc)
        total = ssm[pl.ds(pl.multiple_of(c * 16, 16), 16), :] + sc[...]
        for k in range(4):
            sa[k] = total[:, 256 * k : 256 * k + 256]
        for k in (2, 1, 3):
            start(G_S1, sa.at[lax.rem(x + k, 4)], sb1.at[k - 1], dev(x + k, y, z, c))

    def m2():
        arrived(G_S1, sb1)
        total = sa[x] + sb1[0] + sb1[1] + sb1[2]
        for k in range(4):
            spt[k] = total[8 * (k // 2) : 8 * (k // 2) + 8, 128 * (k % 2) : 128 * (k % 2) + 128]
        for k in (2, 1, 3):
            start(G_S2, spt.at[lax.rem(y + k, 4)], sb2.at[k - 1], dev(x, y + k, z, c))

    def m3():
        arrived(G_S2, sb2)
        sz[z] = spt[y] + sb2[0] + sb2[1] + sb2[2]
        for k in (4, 3, 5, 2, 6, 1, 7):
            start(G_S3, sz.at[z], sz.at[z], dev(x, y, z + k, c))

    def m5():
        arrived(G_S3, b3.at[0])
        sy[y] = jnp.sum(sz[...], axis=0)
        for k in (2, 1, 3):
            start(G_S5, sy.at[y], sy.at[y], dev(x, y + k, z, c))

    def m6():
        arrived(G_S5, sb2)
        for k in range(4):
            sx[x, 8 * (k // 2) : 8 * (k // 2) + 8, 128 * (k % 2) : 128 * (k % 2) + 128] = sy[k]
        for k in (2, 1, 3):
            start(G_S6, sx.at[x], sx.at[x], dev(x + k, y, z, c))

    def m7():
        arrived(G_S6, sb1)
        start(G_S7, sx, sxo, sibling)

    def m8():
        arrived(G_S7, sc)
        for k in range(4):
            sm_out[pl.ds(pl.multiple_of(c * 16, 16), 16), 256 * k : 256 * k + 256] = sx[k]
            sm_out[pl.ds(pl.multiple_of((1 - c) * 16, 16), 16), 256 * k : 256 * k + 256] = sxo[k]

    def returned():
        arrived(G_RZ, u2.at[pl.ds(0, 7)])
        for k in range(8):
            t2[k] = u2[:, k, :]
        for k in range(1, 8):
            px, pc = lax.rem(x + k // 2, NX_), lax.rem(c + k % 2, NC_)
            start(G_RX, t2.at[px * 2 + pc], bk.at[xc], dev(px, y, z, pc))
        bk[xc] = t2[xc]

    def particles():
        arrived(G_RX, bk.at[pl.ds(0, 7)])
        rows = jnp.concatenate(three(bk[...].reshape(64, 128)), 1).astype(BF16)
        at = tn(rows, member16)
        at = jnp.where(jnp.concatenate([mine] * 3, 0), at, 0.0)
        at = fold(at)
        po[9:12, :] = jnp.where(live, pk[6:7, :] * at, 0.0)
        po[12:13, :] = jnp.where(live, jnp.sum(pk[3:6, :] * at, axis=0, keepdims=True), 0.0)

    def velocity_bar():
        arrived(G_H2, r1)
        for k in range(4):
            cols = slice(128 * k, 128 * k + 128)
            dz, dy = difference(fb4, hz2, hy2, k)
            dx = along_x(bar[:, cols])
            for i in range(3):
                total = dz[3 * i : 3 * i + 1] + dy[3 * i + 1 : 3 * i + 2] + dx[3 * i + 2 : 3 * i + 3]
                po[6 + i : 7 + i, cols] = -total

    s2(0)
    s2(1)
    m1()
    returned()
    velocity_bar()
    s3(0)
    s3(1)
    s2(2)
    s2(3)
    m2()
    particles()
    s4(0)
    s4(1)
    s3(2)
    s3(3)
    m3()
    s5(0)
    s5(1)
    s4(2)
    s4(3)
    m5()
    s6(0)
    s6(1)
    s5(2)
    s5(3)
    m6()
    s6(2)
    s6(3)
    m7()
    left(G_P1, r1.at[pl.ds(0, 7)])
    left(G_P2, r1.at[pl.ds(0, 7)])
    left(G_H1, r1)
    left(G_H2, r1)
    left(G_RZ, r1.at[pl.ds(0, 7)])
    left(G_RX, r1.at[pl.ds(0, 7)])
    left(G_SC, sc)
    left(G_S1, sb1)
    left(G_S2, sb2)
    left(G_S3, b3.at[0])
    left(G_S5, sb2)
    left(G_S6, sb1)
    for q in range(NBLK):
        left(B_CORE + q, cb.at[q])
        left(B_R1 + q, b1.at[q])
        left(B_R2 + q, b2.at[q])
        left(B_RZ + q, b3.at[q])
        left(B_GZ + q, b3.at[q])
        left(B_G2 + q, b2.at[q])
    s7(0)
    s7(1)
    m8()
    left(G_S7, sc)
    for q in range(2, NBLK):
        s7(q)
    for q in range(NBLK):
        s8(q)
        left(B_G1 + q, b1.at[q])
        left(B_FO + q, p2.at[q])
        left(B_FR + q, b1.at[q])


def finish(sm, po, stress, vbar, slip, rate, gin, gbin, gbmid, gout):
    for k in range(4):
        cols = slice(128 * k, 128 * k + 128)
        for i in range(6):
            stress[i, k // 2, k % 2 : k % 2 + 1, :] = po[i : i + 1, cols]
        for i in range(3):
            vbar[i, k // 2, k % 2 : k % 2 + 1, :] = po[6 + i : 7 + i, cols]
    slip[...] = po[9:12, :]
    rate[...] = po[12:13, :]
    gin[...] = sm[0:12, :]
    gbin[...] = sm[12:13, :]
    gbmid[...] = sm[22:23, :]
    gout[...] = sm[16:22, :]


def tiles(*shape, dtype=F32):
    return pltpu.VMEM(shape, dtype)


def shards(velocity, slip, rate, owner, cell, count, w_in, b_in, w_mid, b_mid, w_out, tau_bar):
    packed = jnp.concatenate(
        [
            velocity.reshape(3, CELLS),
            slip,
            rate.reshape(1, SLOTS),
            cell.astype(F32).reshape(1, SLOTS),
            tau_bar.astype(F32).reshape(6, CELLS),
            owner.astype(F32).reshape(1, SLOTS),
            jnp.zeros((1, CELLS), F32),
        ],
        0,
    )
    vmem = pl.BlockSpec(memory_space=pltpu.VMEM)
    big, sm, po = pl.pallas_call(
        body,
        name="adjoint",
        out_shape=(
            pltpu.VMEM((HID, HID), F32),
            pltpu.VMEM((32, HID), F32),
            pltpu.VMEM((16, CELLS), F32),
        ),
        in_specs=[
            vmem,
            pl.BlockSpec(memory_space=pltpu.SMEM),
            vmem,
            vmem,
            pl.BlockSpec(memory_space=pl.ANY),
            vmem,
            vmem,
        ],
        out_specs=(vmem, vmem, vmem),
        scratch_shapes=[
            tiles(HID, HID, dtype=BF16),
            tiles(16, HID),
            tiles(16, HID),
            tiles(4, 8, 128),
            tiles(2, 2, 8, 128),
            tiles(2, 2, 8, 128),
            tiles(16, CELLS),
            tiles(8, 8, 128),
            tiles(8, 8, 128),
            tiles(8, 8, 128),
            tiles(8, 8, 128),
            tiles(64 * CAP, CELLS, dtype=BF16),
            tiles(64 * CAP, 384, dtype=BF16),
            tiles(CELLS, HID),
            tiles(HID, CELLS, dtype=BF16),
            tiles(CELLS, HID, dtype=BF16),
            tiles(CELLS, HID),
            tiles(CELLS, HID, dtype=BF16),
            tiles(CELLS, HID, dtype=BF16),
            tiles(CELLS, HID, dtype=BF16),
            tiles(NBLK, HID // 2, BLK),
            tiles(NBLK, HID // 2, BLK),
            tiles(NBLK, HID // 2, BLK),
            tiles(NBLK, 3, 128, BLK),
            tiles(NBLK, 128, BLK),
            tiles(NBLK, 3, 32, BLK),
            tiles(NBLK, 8, 8, 128),
            tiles(NBLK, 7, 8, 128),
            tiles(NBLK, 8, 8, 128),
            tiles(NBLK, 128, BLK),
            tiles(32, HID),
            tiles(16, HID),
            tiles(4, 16, 256),
            tiles(3, 16, 256),
            tiles(4, 8, 128),
            tiles(3, 8, 128),
            tiles(8, 8, 128),
            tiles(4, 8, 128),
            tiles(4, 16, 256),
            tiles(4, 16, 256),
            tiles(4, 8, 128),
            tiles(2, 2, 8, 128),
            tiles(2, 2, 8, 128),
            tiles(8, 8, 128),
            tiles(8, 8, 128),
            tiles(8, 8, 128),
            tiles(8, 8, 128),
            pltpu.SemaphoreType.DMA((N_SEMS,)),
            pltpu.SemaphoreType.DMA((N_SEMS,)),
            pltpu.SemaphoreType.DMA((1,)),
        ],
        compiler_params=pltpu.CompilerParams(
            collective_id=0, has_side_effects=True, vmem_limit_bytes=48 << 20
        ),
    )(packed, count, w_in, b_in.reshape(1, HID), w_mid, b_mid.reshape(1, HID), w_out.T)
    out = [
        jax.ShapeDtypeStruct(s, F32)
        for s in (
            (6, 2, 2, 128),
            (3, 2, 2, 128),
            (3, SLOTS),
            (1, SLOTS),
            (12, HID),
            (1, HID),
            (1, HID),
            (6, HID),
        )
    ]
    stress, vbar, slip_bar, rate_bar, gin, gbin, gbmid, gout = pl.pallas_call(
        finish,
        name="finish",
        out_shape=out,
        in_specs=[vmem, vmem],
        out_specs=[vmem] * 8,
        compiler_params=pltpu.CompilerParams(vmem_limit_bytes=4 << 20),
    )(sm, po)
    return (
        stress,
        vbar,
        slip_bar,
        rate_bar.reshape(SLOTS),
        gin,
        gbin.reshape(HID),
        big,
        gbmid.reshape(HID),
        gout.T,
    )


def solution(mesh):
    return jax.shard_map(
        shards,
        mesh=mesh,
        in_specs=(
            P(None, "gz", "gy", None),
            P(None, ("gz", "gy")),
            P(("gz", "gy")),
            P(("gz", "gy"), None),
            P(("gz", "gy")),
            P(("gz", "gy")),
            P(),
            P(),
            P(),
            P(),
            P(),
            P(None, "gz", "gy", None),
        ),
        out_specs=(
            P(None, "gz", "gy", None),
            P(None, "gz", "gy", None),
            P(None, ("gz", "gy")),
            P(("gz", "gy")),
            P(),
            P(),
            P(),
            P(),
            P(),
        ),
        check_vma=False,
    )
```

time: 602 us -> 83.4 us (0.14)
  waiting for transfers between devices: 497 us -> 0 us
  Pallas kernels: 0 us -> 73.3 us
  starting transfers between devices: 42.3 us -> 0 us
  local copies, waits for them, and re-layouts: 24.4 us -> 7 us
  between operations: 15 us -> 1.31 us
  matrix products: 13.5 us -> 0 us
  other arithmetic: 8.1 us -> 1.37 us
    psum x2 -> x0, waiting for transfers between devices: 481 us -> none  [shards(): lax.psum((grad_w_in, grad_b_in, grad_w_mid, grad_b_mid, grad_w_out), ('gz...]
    pallas_call x0 -> x2, Pallas kernels: none -> 73.3 us  [the longest x1 72.6 us: shards(): pl.pallas_call(body, name='adjoint', out_shape=(pltpu.VMEM((HID, HID), F3...]
    all_to_all x3 -> x0, starting transfers between devices: 31.5 us -> none  [the longest x1 12.6 us: shards(): lax.all_to_all(send_cell, 'gz', split_axis=1, concat_axis=1, tiled=True)]
    all_to_all x3 -> x0, waiting for transfers between devices: 16 us -> none  [the longest x1 8.7 us: shards(): lax.all_to_all(send_force, 'gz', split_axis=1, concat_axis=1, tiled=True)]
    dot_general x11 -> x0, matrix products: 13.5 us -> none  [the longest x1 3.35 us: shards(): jnp.einsum('gc,hc->gh', hidden_one, delta_two, preferred_element_type=jnp...]
    ppermute x8 -> x0, starting transfers between devices: 10.5 us -> none  [the longest x4 8.79 us: with_halo(): lax.ppermute(head, axis, [((i + 1) % count, i) for i in range(count)])]
  transfers between devices with their start and end apart: 13 -> 0, of which waited for: 4 -> 0; matrix products, arithmetic and copies ran while one was open for 4% -> 0% of each run, Pallas kernels for 0% -> 0%
where the time goes in v1:
time: 83.4 us; the launch traced here: 82.9 us
  Pallas kernels  73.3 us (88%)
  local copies, waits for them, and re-layouts  7 us (8%)
  other arithmetic  1.37 us (2%)
  between operations  1.31 us (2%)
    pallas_call x1, Pallas kernels, shards(): pl.pallas_call(body, name='adjoint', out_shape=(pltpu.VMEM((HID, HID), F3...  72.6 us
    unnamed x9, local copies, waits for them, and re-layouts  4.86 us

profile of v1, /device:TPU:1, one launch (start us, length us, event | category | flops | bytes accessed | tf_op | source)
XLA Modules:
  0.0 82.9 jit_solution(5856166612132735888)
XLA Ops:
  1.3 0.7 convert_bitcast_fusion
  2.0 0.7 convert_element_type.7
  2.7 0.7 reshape.51
  3.4 0.7 reshape.63
  4.1 0.7 concatenate.3.pk
  4.8 0.0 copy-start
  4.8 0.8 copy-done
  5.6 0.0 copy-start.1
  5.6 0.7 copy-done.1
  6.3 0.0 copy-start.2
  6.3 0.7 copy-done.2
  7.0 0.0 copy-start.3
  7.0 0.7 copy-done.3
  7.7 72.6 %adjoint.1 = (f32[1024,1024]{1,0:T(8,128)S(1)}, f32[32,1024]{1,0:T(8,128)S(1)}, f32[16,512]{1,0:T(8,128)S(1)}) custom-call(f32[16,512]{1,0:T(8,128)S(1)} %concatenate.3.pk, s32[1]{0:T(128)S(6)} %copy.23.cnt, bf16[12,1024]{1,0:T(8,128)(2,1)S(1)} %copy-done, f32[1,1024]{1,0:T(1,128)S(1)} %bitcast.12, bf16[1024,1024]{1,0:T(8,128)(2,1)} %w_mid_any.1, ...), custom_call_target="tpu_custom_call" | custom-call | tf_op jit(solution)/shard_map/adjoint/pallas_call | solution.py:573
  80.2 0.7 finish.1
  80.9 2.0 %copy.22 = f32[1024,1024]{1,0:T(8,128)} copy(f32[1024,1024]{1,0:T(8,128)S(1)} %get-tuple-element.37) | data formatting | bytes 8388608
  (1 shorter events, 0.0 us)
Async XLA Ops:
  4.8 0.8 copy-start
  5.6 0.7 copy-start.1
  6.3 0.7 copy-start.2
  7.0 0.7 copy-start.3

commit v2 on v1

--- a/solution.py
+++ b/solution.py
@@ -27,8 +27,9 @@
     G_S7,
     G_BIG,
 ) = range(14)
-B_CORE, B_R1, B_R2, B_RZ, B_GZ, B_G2, B_G1, B_FO, B_FR = (G_BIG + NBLK * i for i in range(9))
-N_SEMS = G_BIG + NBLK * 9
+B_CORE, B_RZ, B_GZ, B_FR = (G_BIG + NBLK * i for i in range(4))
+B_R1, B_R2, B_G2, B_G1 = (G_BIG + NBLK * (4 + 2 * i) for i in range(4))
+N_SEMS = G_BIG + NBLK * 12
 
 
 def nn(a, b):
@@ -55,19 +56,35 @@
 
 
 def body(
-    pk,
+    velocity_in,
+    slip_in,
+    rate_in,
+    owner_in,
+    cell_in,
     cnt,
-    w_in,
-    b_in,
-    w_mid_any,
-    b_mid,
-    w_out,
+    w_in_in,
+    b_in_in,
+    w_mid_in,
+    b_mid_in,
+    w_out_in,
+    tau_in,
     out,
     sm_out,
     po,
+    velocity,
+    slip,
+    rate,
+    owner,
+    cell,
+    w_in,
+    b_in,
+    b_mid,
+    w_out,
+    tau_bar,
     w_mid,
     w_in16,
     w_out16,
+    tau_rows,
     v4,
     hz,
     hy,
@@ -145,9 +162,6 @@
     def left(group, whole):
         pltpu.make_async_copy(whole, whole, send.at[group]).wait()
 
-    load_w = pltpu.make_async_copy(w_mid_any, w_mid, local.at[0])
-    load_w.start()
-
     sibling = dev(x, y, z, c + 1)
     partners = [dev(x + k // 2, y, z, c + k % 2) for k in range(1, 8)]
     partners += [dev(x, y + k, z, c) for k in range(1, 4)]
@@ -157,18 +171,42 @@
     for who in partners:
         pl.semaphore_signal(barrier, inc=1, device_id=who, device_id_type=pl.DeviceIdType.MESH)
 
+    loads = [
+        pltpu.make_async_copy(src, dst, local.at[i])
+        for i, (src, dst) in enumerate(
+            (
+                (owner_in, owner),
+                (cell_in, cell),
+                (rate_in, rate),
+                (slip_in, slip),
+                (velocity_in, velocity),
+                (tau_in, tau_bar),
+                (w_in_in, w_in),
+                (w_out_in, w_out),
+                (b_in_in, b_in),
+                (b_mid_in, b_mid),
+                (w_mid_in, w_mid),
+            )
+        )
+    ]
+    for load in loads:
+        load.start()
+
+    for load in loads[0:5]:
+        load.wait()
     for k in range(4):
-        v4[k] = pk[0:8, 128 * k : 128 * k + 128]
+        for i in range(3):
+            v4[k, i : i + 1, :] = velocity[i, k // 2, k % 2 : k % 2 + 1, :]
     lane = iota((1, SLOTS), 1)
     live = lane < cnt[0]
-    owner = pk[14:15, :].astype(I32)
-    row = (owner >> 4) * 16 + (owner & 1) * 8 + ((owner >> 1) & 7)
+    slab = owner[...]
+    row = (slab >> 4) * 16 + (slab & 1) * 8 + ((slab >> 1) & 7)
     member = jnp.where(iota((64, SLOTS), 0) == row, 1.0, 0.0)
     member16 = member.astype(BF16)
     earlier = jnp.where(iota((SLOTS, SLOTS), 0) < iota((SLOTS, SLOTS), 1), 1.0, 0.0).astype(BF16)
     place = jnp.sum(nn(member16, earlier) * member, axis=0, keepdims=True).astype(I32)
-    force = jnp.where(live, pk[6:7, :] * pk[3:6, :], 0.0)
-    four = jnp.concatenate([force, pk[7:8, :]], 0)
+    force = jnp.where(live, rate[...] * slip[...], 0.0)
+    four = jnp.concatenate([force, cell[...].astype(F32)], 0)
     sub = iota((128, SLOTS), 0)
     mine = (sub // 4) == place
     wide = jnp.where(mine, jnp.concatenate([four] * 32, 0), 0.0)
@@ -192,11 +230,20 @@
 
     halo(G_H1, v4, hz, hy)
 
+    for load in loads[5:10]:
+        load.wait()
     w_in16[...] = jnp.zeros_like(w_in16)
     w_in16[0:12, :] = w_in[...].astype(F32)
     w_out16[...] = jnp.zeros_like(w_out16)
     w_out16[0:6, :] = w_out[...].astype(F32)
-    tau = jnp.concatenate([pk[8:14, :], jnp.zeros((10, CELLS), F32)], 0)
+    tau_rows[...] = jnp.zeros_like(tau_rows)
+    for i in range(6):
+        for k in range(2):
+            pair = tau_bar[i, k].astype(F32)
+            for j in range(2):
+                at = 256 * k + 128 * j
+                tau_rows[i : i + 1, at : at + 128] = pair[j : j + 1]
+    tau = tau_rows[...]
     tau16 = tau.astype(BF16)
     tau_one = jnp.where(iota((16, CELLS), 0) == 6, 1.0, tau).astype(BF16)
 
@@ -250,7 +297,7 @@
         return total[0:3] + total[4:7]
 
     feats[9:12, :] = fold(tn(fs[...], onehot[...]))
-    load_w.wait()
+    loads[10].wait()
 
     feats16 = feats[...].astype(BF16)
 
@@ -279,13 +326,13 @@
         return dev(x + k * p, y + k * (1 - p), z, c)
 
     def s1(q):
-        p = lax.rem(q, 2)
         arrived(B_CORE + q, cb.at[q])
-        a1[q] = a1[q] + cb[q]
-        for k in (2, 1, 3):
-            to = lax.rem(me1(p) + k, 4)
-            rows = pl.ds(pl.multiple_of(to * 128, 128), 128)
-            start(B_R1 + q, a1.at[q, rows], b1.at[q, k - 1], peer1(p, k))
+        for p in range(2):
+            a1[q, p] = a1[q, p] + cb[q, :, 128 * p : 128 * p + 128]
+            for k in (2, 1, 3):
+                to = lax.rem(me1(p) + k, 4)
+                rows = pl.ds(pl.multiple_of(to * 128, 128), 128)
+                start(B_R1 + 2 * q + p, a1.at[q, p, rows], b1.at[q, p, k - 1], peer1(p, k))
 
     half = HID // 2
 
@@ -299,18 +346,145 @@
         g2t[:, cols] = delta
         cs[q] = nn(h1[pl.ds(pl.multiple_of((1 - c) * half, half), half), :], delta)
         start(B_CORE + q, cs.at[q], cb.at[q], sibling)
-        a1[q] = nn(h1[pl.ds(pl.multiple_of(c * half, half), half), :], delta)
+        own = nn(h1[pl.ds(pl.multiple_of(c * half, half), half), :], delta)
+        a1[q, 0] = own[:, 0:128]
+        a1[q, 1] = own[:, 128:256]
         by_hidden, by_delta = nn(tau_one, hidden), nn(tau_one, delta)
         ssm[16:32, cols] = jnp.where(iota((16, BLK), 0) == 6, by_delta, by_hidden)
 
-        @pl.when(q > 0)
+        @pl.when((q == 1) | (q == 2))
         def _():
             s1(q - 1)
 
         return carry
 
     lax.fori_loop(0, NBLK, second, 0)
-    s1(NBLK - 1)
+
+    def s2(q):
+        for p in range(2):
+            arrived(B_R1 + 2 * q + p, b1.at[q, p])
+            own = a1[q, p, pl.ds(pl.multiple_of(me1(p) * 128, 128), 128), :]
+            p2[q, p] = own + b1[q, p, 0] + b1[q, p, 1] + b1[q, p, 2]
+            for k in (2, 1, 3):
+                rows = pl.ds(pl.multiple_of(lax.rem(me2(p) + k, 4) * 32, 32), 32)
+                start(B_R2 + 2 * q + p, p2.at[q, p, rows], b2.at[q, p, k - 1], peer2(p, k))
+
+    def s3(q):
+        for p in range(2):
+            arrived(B_R2 + 2 * q + p, b2.at[q, p])
+            own = p2[q, p, pl.ds(pl.multiple_of(me2(p) * 32, 32), 32), :]
+            total = own + b2[q, p, 0] + b2[q, p, 1] + b2[q, p, 2]
+            for k in range(8):
+                p3[q, k, 4 * p : 4 * p + 4, :] = total[4 * k : 4 * k + 4]
+        for k in (4, 3, 5, 2, 6, 1, 7):
+            pz = lax.rem(z + k, NZ_)
+            start(B_RZ + q, p3.at[q, pz], b3.at[q, k - 1], dev(x, y, pz, c))
+
+    def s4(q):
+        arrived(B_RZ + q, b3.at[q])
+        zz[q, z] = p3[q, z] + jnp.sum(b3[q], axis=0)
+        for k in (4, 3, 5, 2, 6, 1, 7):
+            start(B_GZ + q, zz.at[q, z], zz.at[q, z], dev(x, y, z + k, c))
+
+    def s5(q):
+        arrived(B_GZ + q, b3.at[q])
+        for p in range(2):
+            rows = pl.ds(pl.multiple_of(me2(p) * 32, 32), 32)
+            y2[q, p, rows, :] = jnp.concatenate([zz[q, k, 4 * p : 4 * p + 4, :] for k in range(8)], 0)
+            piece = y2.at[q, p, rows]
+            for k in (2, 1, 3):
+                start(B_G2 + 2 * q + p, piece, piece, peer2(p, k))
+
+    def s6(q):
+        for p in range(2):
+            arrived(B_G2 + 2 * q + p, b2.at[q, p])
+            rows = pl.ds(pl.multiple_of(c * half + me1(p) * 128, 128), 128)
+            cols = slice(BLK * q + 128 * p, BLK * q + 128 * p + 128)
+            for k in (2, 1, 3):
+                start(B_G1 + 2 * q + p, y2.at[q, p], out.at[rows, cols], peer1(p, k))
+            out[rows, cols] = y2[q, p]
+
+    def s7(q):
+        for p in range(2):
+            arrived(B_G1 + 2 * q + p, b1.at[q, p])
+        where = out.at[pl.ds(pl.multiple_of(c * half, half), half), BLK * q : BLK * q + BLK]
+        start(B_FR + q, where, where, sibling)
+
+    def s8(q):
+        arrived(B_FR + q, cb.at[q])
+
+    def m1():
+        arrived(G_SC, sc)
+        total = ssm[pl.ds(pl.multiple_of(c * 16, 16), 16), :] + sc[...]
+        for k in range(4):
+            sa[k] = total[:, 256 * k : 256 * k + 256]
+        for k in (2, 1, 3):
+            start(G_S1, sa.at[lax.rem(x + k, 4)], sb1.at[k - 1], dev(x + k, y, z, c))
+
+    def m2():
+        arrived(G_S1, sb1)
+        total = sa[x] + sb1[0] + sb1[1] + sb1[2]
+        for k in range(4):
+            spt[k] = total[8 * (k // 2) : 8 * (k // 2) + 8, 128 * (k % 2) : 128 * (k % 2) + 128]
+        for k in (2, 1, 3):
+            start(G_S2, spt.at[lax.rem(y + k, 4)], sb2.at[k - 1], dev(x, y + k, z, c))
+
+    def m3():
+        arrived(G_S2, sb2)
+        sz[z] = spt[y] + sb2[0] + sb2[1] + sb2[2]
+        for k in (4, 3, 5, 2, 6, 1, 7):
+            start(G_S3, sz.at[z], sz.at[z], dev(x, y, z + k, c))
+
+    def m5():
+        arrived(G_S3, b3.at[0])
+        sy[y] = jnp.sum(sz[...], axis=0)
+        for k in (2, 1, 3):
+            start(G_S5, sy.at[y], sy.at[y], dev(x, y + k, z, c))
+
+    def m6():
+        arrived(G_S5, sb2)
+        for k in range(4):
+            sx[x, 8 * (k // 2) : 8 * (k // 2) + 8, 128 * (k % 2) : 128 * (k % 2) + 128] = sy[k]
+        for k in (2, 1, 3):
+            start(G_S6, sx.at[x], sx.at[x], dev(x + k, y, z, c))
+
+    def m7():
+        arrived(G_S6, sb1)
+        start(G_S7, sx, sxo, sibling)
+
+    def m8():
+        arrived(G_S7, sc)
+        for k in range(4):
+            sm_out[pl.ds(pl.multiple_of(c * 16, 16), 16), 256 * k : 256 * k + 256] = sx[k]
+            sm_out[pl.ds(pl.multiple_of((1 - c) * 16, 16), 16), 256 * k : 256 * k + 256] = sxo[k]
+
+    def returned():
+        arrived(G_RZ, u2.at[pl.ds(0, 7)])
+        for k in range(8):
+            t2[k] = u2[:, k, :]
+        for k in range(1, 8):
+            px, pc = lax.rem(x + k // 2, NX_), lax.rem(c + k % 2, NC_)
+            start(G_RX, t2.at[px * 2 + pc], bk.at[xc], dev(px, y, z, pc))
+        bk[xc] = t2[xc]
+
+    def particles():
+        arrived(G_RX, bk.at[pl.ds(0, 7)])
+        rows = jnp.concatenate(three(bk[...].reshape(64, 128)), 1).astype(BF16)
+        at = tn(rows, member16)
+        at = jnp.where(jnp.concatenate([mine] * 3, 0), at, 0.0)
+        at = fold(at)
+        po[9:12, :] = jnp.where(live, rate[...] * at, 0.0)
+        po[12:13, :] = jnp.where(live, jnp.sum(slip[...] * at, axis=0, keepdims=True), 0.0)
+
+    def velocity_bar():
+        arrived(G_H2, r1)
+        for k in range(4):
+            cols = slice(128 * k, 128 * k + 128)
+            dz, dy = difference(fb4, hz2, hy2, k)
+            dx = along_x(bar[:, cols])
+            for i in range(3):
+                total = dz[3 * i : 3 * i + 1] + dy[3 * i + 1 : 3 * i + 2] + dx[3 * i + 2 : 3 * i + 3]
+                po[6 + i : 7 + i, cols] = -total
 
     def third(q, carry):
         cols = pl.ds(pl.multiple_of(q * BLK, BLK), BLK)
@@ -322,10 +496,14 @@
     lax.fori_loop(0, NBLK, third, 0)
     start(G_SC, ssm.at[pl.ds(pl.multiple_of((1 - c) * 16, 16), 16)], sc, sibling)
 
+    s2(0)
+    s1(2)
     bar = nt(w_in16[...].astype(BF16), g1t[...])
     for k in range(4):
         fb4[k] = bar[0:8, 128 * k : 128 * k + 128]
     halo(G_H2, fb4, hz2, hy2)
+    s2(1)
+    s1(3)
     spread = jnp.concatenate([bar[9:12], jnp.zeros((1, CELLS), F32)], 0)
     spread = jnp.concatenate([spread] * 32, 0)
     picked = nt(onehot[...], jnp.concatenate(three(spread), 0).astype(BF16))
@@ -341,170 +519,33 @@
     u2[z] = rts[z]
     po[0:6, :] = nt(w_out16[...].astype(BF16), h2t[...])[0:6]
 
-    def s2(q):
-        p = q % 2
-        arrived(B_R1 + q, b1.at[q])
-        own = a1[q, pl.ds(pl.multiple_of(me1(p) * 128, 128), 128), :]
-        p2[q] = own + b1[q, 0] + b1[q, 1] + b1[q, 2]
-        for k in (2, 1, 3):
-            to = lax.rem(me2(p) + k, 4)
-            start(
-                B_R2 + q, p2.at[q, pl.ds(pl.multiple_of(to * 32, 32), 32)], b2.at[q, k - 1], peer2(p, k)
-            )
-
-    def s3(q):
-        p = q % 2
-        arrived(B_R2 + q, b2.at[q])
-        own = p2[q, pl.ds(pl.multiple_of(me2(p) * 32, 32), 32), :]
-        total = own + b2[q, 0] + b2[q, 1] + b2[q, 2]
-        for k in range(8):
-            r, cc = k // 2, k % 2
-            p3[q, k] = total[8 * r : 8 * r + 8, 128 * cc : 128 * cc + 128]
-        for k in (4, 3, 5, 2, 6, 1, 7):
-            pz = lax.rem(z + k, NZ_)
-            start(B_RZ + q, p3.at[q, pz], b3.at[q, k - 1], dev(x, y, pz, c))
-
-    def s4(q):
-        arrived(B_RZ + q, b3.at[q])
-        zz[q, z] = p3[q, z] + jnp.sum(b3[q], axis=0)
-        for k in (4, 3, 5, 2, 6, 1, 7):
-            start(B_GZ + q, zz.at[q, z], zz.at[q, z], dev(x, y, z + k, c))
-
-    def s5(q):
-        p = q % 2
-        arrived(B_GZ + q, b3.at[q])
-        own = pl.multiple_of(me2(p) * 32, 32)
-        for k in range(8):
-            r, cc = k // 2, k % 2
-            y2[q, pl.ds(own + 8 * r, 8), 128 * cc : 128 * cc + 128] = zz[q, k]
-        piece = y2.at[q, pl.ds(own, 32)]
-        for k in (2, 1, 3):
-            start(B_G2 + q, piece, piece, peer2(p, k))
-
-    def region(q, core, d1):
-        return out.at[pl.ds(pl.multiple_of(core * half + d1 * 128, 128), 128), BLK * q : BLK * q + BLK]
-
-    def s6(q):
-        p = q % 2
-        arrived(B_G2 + q, b2.at[q])
-        for k in (2, 1, 3):
-            start(B_G1 + q, y2.at[q], region(q, c, me1(p)), peer1(p, k))
-        start(B_FO + q, y2.at[q], region(q, c, me1(p)), sibling)
-        out[pl.ds(pl.multiple_of(c * half + me1(p) * 128, 128), 128), BLK * q : BLK * q + BLK] = y2[q]
-
-    def s7(q):
-        p = q % 2
-        arrived(B_G1 + q, b1.at[q])
-        for k in (1, 2, 3):
-            where = region(q, c, lax.rem(me1(p) + k, 4))
-            start(B_FR + q, where, where, sibling)
-
-    def s8(q):
-        arrived(B_FO + q, p2.at[q])
-        arrived(B_FR + q, b1.at[q])
-
-    def m1():
-        arrived(G_SC, sc)
-        total = ssm[pl.ds(pl.multiple_of(c * 16, 16), 16), :] + sc[...]
-        for k in range(4):
-            sa[k] = total[:, 256 * k : 256 * k + 256]
-        for k in (2, 1, 3):
-            start(G_S1, sa.at[lax.rem(x + k, 4)], sb1.at[k - 1], dev(x + k, y, z, c))
-
-    def m2():
-        arrived(G_S1, sb1)
-        total = sa[x] + sb1[0] + sb1[1] + sb1[2]
-        for k in range(4):
-            spt[k] = total[8 * (k // 2) : 8 * (k // 2) + 8, 128 * (k % 2) : 128 * (k % 2) + 128]
-        for k in (2, 1, 3):
-            start(G_S2, spt.at[lax.rem(y + k, 4)], sb2.at[k - 1], dev(x, y + k, z, c))
-
-    def m3():
-        arrived(G_S2, sb2)
-        sz[z] = spt[y] + sb2[0] + sb2[1] + sb2[2]
-        for k in (4, 3, 5, 2, 6, 1, 7):
-            start(G_S3, sz.at[z], sz.at[z], dev(x, y, z + k, c))
-
-    def m5():
-        arrived(G_S3, b3.at[0])
-        sy[y] = jnp.sum(sz[...], axis=0)
-        for k in (2, 1, 3):
-            start(G_S5, sy.at[y], sy.at[y], dev(x, y + k, z, c))
-
-    def m6():
-        arrived(G_S5, sb2)
-        for k in range(4):
-            sx[x, 8 * (k // 2) : 8 * (k // 2) + 8, 128 * (k % 2) : 128 * (k % 2) + 128] = sy[k]
-        for k in (2, 1, 3):
-            start(G_S6, sx.at[x], sx.at[x], dev(x + k, y, z, c))
-
-    def m7():
-        arrived(G_S6, sb1)
-        start(G_S7, sx, sxo, sibling)
-
-    def m8():
-        arrived(G_S7, sc)
-        for k in range(4):
-            sm_out[pl.ds(pl.multiple_of(c * 16, 16), 16), 256 * k : 256 * k + 256] = sx[k]
-            sm_out[pl.ds(pl.multiple_of((1 - c) * 16, 16), 16), 256 * k : 256 * k + 256] = sxo[k]
-
-    def returned():
-        arrived(G_RZ, u2.at[pl.ds(0, 7)])
-        for k in range(8):
-            t2[k] = u2[:, k, :]
-        for k in range(1, 8):
-            px, pc = lax.rem(x + k // 2, NX_), lax.rem(c + k % 2, NC_)
-            start(G_RX, t2.at[px * 2 + pc], bk.at[xc], dev(px, y, z, pc))
-        bk[xc] = t2[xc]
-
-    def particles():
-        arrived(G_RX, bk.at[pl.ds(0, 7)])
-        rows = jnp.concatenate(three(bk[...].reshape(64, 128)), 1).astype(BF16)
-        at = tn(rows, member16)
-        at = jnp.where(jnp.concatenate([mine] * 3, 0), at, 0.0)
-        at = fold(at)
-        po[9:12, :] = jnp.where(live, pk[6:7, :] * at, 0.0)
-        po[12:13, :] = jnp.where(live, jnp.sum(pk[3:6, :] * at, axis=0, keepdims=True), 0.0)
-
-    def velocity_bar():
-        arrived(G_H2, r1)
-        for k in range(4):
-            cols = slice(128 * k, 128 * k + 128)
-            dz, dy = difference(fb4, hz2, hy2, k)
-            dx = along_x(bar[:, cols])
-            for i in range(3):
-                total = dz[3 * i : 3 * i + 1] + dy[3 * i + 1 : 3 * i + 2] + dx[3 * i + 2 : 3 * i + 3]
-                po[6 + i : 7 + i, cols] = -total
-
-    s2(0)
-    s2(1)
+    s3(0)
     m1()
     returned()
+    s2(2)
+    s3(1)
     velocity_bar()
-    s3(0)
-    s3(1)
-    s2(2)
     s2(3)
+    s4(0)
+    s3(2)
     m2()
+    s4(1)
+    s3(3)
     particles()
-    s4(0)
-    s4(1)
-    s3(2)
-    s3(3)
+    s5(0)
     m3()
-    s5(0)
+    s4(2)
     s5(1)
-    s4(2)
+    s6(0)
     s4(3)
-    m5()
-    s6(0)
     s6(1)
     s5(2)
+    m5()
     s5(3)
+    s6(2)
     m6()
-    s6(2)
     s6(3)
-    m7()
+    s7(0)
     left(G_P1, r1.at[pl.ds(0, 7)])
     left(G_P2, r1.at[pl.ds(0, 7)])
     left(G_H1, r1)
@@ -516,28 +557,36 @@
     left(G_S2, sb2)
     left(G_S3, b3.at[0])
     left(G_S5, sb2)
-    left(G_S6, sb1)
     for q in range(NBLK):
         left(B_CORE + q, cb.at[q])
-        left(B_R1 + q, b1.at[q])
-        left(B_R2 + q, b2.at[q])
         left(B_RZ + q, b3.at[q])
         left(B_GZ + q, b3.at[q])
-        left(B_G2 + q, b2.at[q])
-    s7(0)
+        for p in range(2):
+            left(B_R1 + 2 * q + p, b1.at[q, p])
+            left(B_R2 + 2 * q + p, b2.at[q, p])
+            left(B_G2 + 2 * q + p, b2.at[q, p])
     s7(1)
+    m7()
+    s7(2)
     m8()
+    left(G_S6, sb1)
     left(G_S7, sc)
-    for q in range(2, NBLK):
-        s7(q)
+    s7(3)
+    for q in range(NBLK):
+        for p in range(2):
+            left(B_G1 + 2 * q + p, b1.at[q, p])
     for q in range(NBLK):
         s8(q)
-        left(B_G1 + q, b1.at[q])
-        left(B_FO + q, p2.at[q])
-        left(B_FR + q, b1.at[q])
-
-
-def finish(sm, po, stress, vbar, slip, rate, gin, gbin, gbmid, gout):
+        left(B_FR + q, cb.at[q])
+
+
+def finish(big, sm, po, stress, vbar, slip, rate, gin, gbin, gmid, gbmid, gout, sem):
+    copies = [
+        pltpu.make_async_copy(big.at[pl.ds(128 * k, 128)], gmid.at[pl.ds(128 * k, 128)], sem.at[k])
+        for k in range(8)
+    ]
+    for copy in copies:
+        copy.start()
     for k in range(4):
         cols = slice(128 * k, 128 * k + 128)
         for i in range(6):
@@ -550,26 +599,25 @@
     gbin[...] = sm[12:13, :]
     gbmid[...] = sm[22:23, :]
     gout[...] = sm[16:22, :]
+    for copy in copies:
+        copy.wait()
 
 
 def tiles(*shape, dtype=F32):
     return pltpu.VMEM(shape, dtype)
 
 
+def in_hbm(value):
+    return pltpu.with_memory_space_constraint(value, pltpu.HBM)
+
+
+def in_vmem(value):
+    return pltpu.with_memory_space_constraint(value, pltpu.VMEM)
+
+
 def shards(velocity, slip, rate, owner, cell, count, w_in, b_in, w_mid, b_mid, w_out, tau_bar):
-    packed = jnp.concatenate(
-        [
-            velocity.reshape(3, CELLS),
-            slip,
-            rate.reshape(1, SLOTS),
-            cell.astype(F32).reshape(1, SLOTS),
-            tau_bar.astype(F32).reshape(6, CELLS),
-            owner.astype(F32).reshape(1, SLOTS),
-            jnp.zeros((1, CELLS), F32),
-        ],
-        0,
-    )
     vmem = pl.BlockSpec(memory_space=pltpu.VMEM)
+    hbm = pl.BlockSpec(memory_space=pltpu.HBM)
     big, sm, po = pl.pallas_call(
         body,
         name="adjoint",
@@ -578,20 +626,23 @@
             pltpu.VMEM((32, HID), F32),
             pltpu.VMEM((16, CELLS), F32),
         ),
-        in_specs=[
-            vmem,
-            pl.BlockSpec(memory_space=pltpu.SMEM),
-            vmem,
-            vmem,
-            pl.BlockSpec(memory_space=pl.ANY),
-            vmem,
-            vmem,
-        ],
+        in_specs=[pl.BlockSpec(memory_space=pltpu.SMEM) if i == 5 else hbm for i in range(12)],
         out_specs=(vmem, vmem, vmem),
         scratch_shapes=[
+            tiles(3, 2, 2, 128),
+            tiles(3, SLOTS),
+            tiles(1, SLOTS),
+            tiles(1, SLOTS, dtype=I32),
+            tiles(1, SLOTS, dtype=I32),
+            tiles(12, HID, dtype=BF16),
+            tiles(1, HID),
+            tiles(1, HID),
+            tiles(6, HID, dtype=BF16),
+            tiles(6, 2, 2, 128, dtype=BF16),
             tiles(HID, HID, dtype=BF16),
             tiles(16, HID),
             tiles(16, HID),
+            tiles(16, CELLS),
             tiles(4, 8, 128),
             tiles(2, 2, 8, 128),
             tiles(2, 2, 8, 128),
@@ -611,14 +662,14 @@
             tiles(CELLS, HID, dtype=BF16),
             tiles(NBLK, HID // 2, BLK),
             tiles(NBLK, HID // 2, BLK),
-            tiles(NBLK, HID // 2, BLK),
-            tiles(NBLK, 3, 128, BLK),
-            tiles(NBLK, 128, BLK),
-            tiles(NBLK, 3, 32, BLK),
+            tiles(NBLK, 2, HID // 2, 128),
+            tiles(NBLK, 2, 3, 128, 128),
+            tiles(NBLK, 2, 128, 128),
+            tiles(NBLK, 2, 3, 32, 128),
             tiles(NBLK, 8, 8, 128),
             tiles(NBLK, 7, 8, 128),
             tiles(NBLK, 8, 8, 128),
-            tiles(NBLK, 128, BLK),
+            tiles(NBLK, 2, 128, 128),
             tiles(32, HID),
             tiles(16, HID),
             tiles(4, 16, 256),
@@ -638,12 +689,25 @@
             tiles(8, 8, 128),
             pltpu.SemaphoreType.DMA((N_SEMS,)),
             pltpu.SemaphoreType.DMA((N_SEMS,)),
-            pltpu.SemaphoreType.DMA((1,)),
+            pltpu.SemaphoreType.DMA((11,)),
         ],
         compiler_params=pltpu.CompilerParams(
             collective_id=0, has_side_effects=True, vmem_limit_bytes=48 << 20
         ),
-    )(packed, count, w_in, b_in.reshape(1, HID), w_mid, b_mid.reshape(1, HID), w_out.T)
+    )(
+        in_hbm(velocity),
+        in_hbm(slip),
+        in_hbm(rate.reshape(1, SLOTS)),
+        in_hbm(owner.T),
+        in_hbm(cell.reshape(1, SLOTS)),
+        count,
+        in_hbm(w_in),
+        in_hbm(b_in.reshape(1, HID)),
+        in_hbm(w_mid),
+        in_hbm(b_mid.reshape(1, HID)),
+        in_hbm(w_out.T),
+        in_hbm(tau_bar),
+    )
     out = [
         jax.ShapeDtypeStruct(s, F32)
         for s in (
@@ -653,18 +717,20 @@
             (1, SLOTS),
             (12, HID),
             (1, HID),
+            (HID, HID),
             (1, HID),
             (6, HID),
         )
     ]
-    stress, vbar, slip_bar, rate_bar, gin, gbin, gbmid, gout = pl.pallas_call(
+    stress, vbar, slip_bar, rate_bar, gin, gbin, gmid, gbmid, gout = pl.pallas_call(
         finish,
         name="finish",
         out_shape=out,
-        in_specs=[vmem, vmem],
-        out_specs=[vmem] * 8,
+        in_specs=[vmem, vmem, vmem],
+        out_specs=[hbm if k == 6 else vmem for k in range(9)],
+        scratch_shapes=[pltpu.SemaphoreType.DMA((8,))],
         compiler_params=pltpu.CompilerParams(vmem_limit_bytes=4 << 20),
-    )(sm, po)
+    )(in_vmem(big), in_vmem(sm), in_vmem(po))
     return (
         stress,
         vbar,
@@ -672,7 +738,7 @@
         rate_bar.reshape(SLOTS),
         gin,
         gbin.reshape(HID),
-        big,
+        gmid,
         gbmid.reshape(HID),
         gout.T,
     )

time: 83.4 us -> 70.7 us (0.85)
  local copies, waits for them, and re-layouts: 7 us -> 0 us
  Pallas kernels: 73.3 us -> 69.3 us
  other arithmetic: 1.37 us -> 0 us
    pallas_call x1, Pallas kernels: 72.6 us -> 66.6 us  [shards(): pl.pallas_call(body, name='adjoint', out_shape=(pltpu.VMEM((HID, HID), F3...]
    unnamed x9 -> x0, local copies, waits for them, and re-layouts: 4.86 us -> none
    pallas_call x1, Pallas kernels: 0.69 us -> 2.73 us  [shards(): pl.pallas_call(finish, name='finish', out_shape=out, in_specs=[vmem, vmem...]
    reshape x2 -> x0, local copies, waits for them, and re-layouts: 1.4 us -> none  [the longest x1 0.71 us: shards(): velocity.reshape(3, CELLS)]
where the time goes in v2:
time: 70.7 us; the launch traced here: 70.6 us
  Pallas kernels  69.3 us (98%)
  between operations  1.3 us (2%)
    pallas_call x1, Pallas kernels, shards(): pl.pallas_call(body, name='adjoint', out_shape=(pltpu.VMEM((HID, HID), F3...  66.6 us
    pallas_call x1, Pallas kernels, shards(): pl.pallas_call(finish, name='finish', out_shape=out, in_specs=[vmem, vmem...  2.73 us

profile of v2, /device:TPU:1, one launch (start us, length us, event | category | flops | bytes accessed | tf_op | source)
XLA Modules:
  0.0 70.6 jit_solution(13731748433312222520)
XLA Ops:
  1.3 66.6 %adjoint.1 = (f32[1024,1024]{1,0:T(8,128)S(1)}, f32[32,1024]{1,0:T(8,128)S(1)}, f32[16,512]{1,0:T(8,128)S(1)}) custom-call(f32[3,2,2,128]{3,2,1,0:T(2,128)} %velocity_in.1, f32[3,512]{1,0:T(4,128)} %slip_in.1, f32[1,512]{1,0:T(1,128)} %bitcast.13, s32[1,512]{1,0:T(1,128)} %bitcast.14, s32[1,512]{1,0:T(1,128)} %bitcast.15, s32[1]{0:T(128)S(6)} %copy.21.cnt, ...), custom_call_target="tpu_custom_call" | custom-call | tf_op jit(solution)/shard_map/adjoint/pallas_call | solution.py:621
  67.9 2.7 %finish.1 = (f32[6,2,2,128]{3,2,1,0:T(2,128)}, f32[3,2,2,128]{3,2,1,0:T(2,128)}, f32[3,512]{1,0:T(4,128)}, f32[1,512]{1,0:T(1,128)}, f32[12,1024]{1,0:T(8,128)},...) custom-call(f32[1024,1024]{1,0:T(8,128)S(1)} %get-tuple-element.21.big, ...), custom_call_target="tpu_custom_call" | custom-call | tf_op jit(solution)/shard_map/finish/pallas_call | solution.py:725

commit v3 on v2

--- a/solution.py
+++ b/solution.py
@@ -27,9 +27,9 @@
     G_S7,
     G_BIG,
 ) = range(14)
-B_CORE, B_RZ, B_GZ, B_FR = (G_BIG + NBLK * i for i in range(4))
-B_R1, B_R2, B_G2, B_G1 = (G_BIG + NBLK * (4 + 2 * i) for i in range(4))
-N_SEMS = G_BIG + NBLK * 12
+B_RZ, B_GZ, B_FR = (G_BIG + NBLK * i for i in range(3))
+B_CORE, B_R1, B_R2, B_G2, B_G1 = (G_BIG + NBLK * (3 + 2 * i) for i in range(5))
+N_SEMS = G_BIG + NBLK * 13
 
 
 def nn(a, b):
@@ -216,7 +216,7 @@
 
     pl.semaphore_wait(barrier, len(partners))
 
-    for k in range(1, 8):
+    for k in (5, 4, 7, 3, 6, 2, 1):
         px, pc = lax.rem(x + k // 2, NX_), lax.rem(c + k % 2, NC_)
         start(G_P1, m_send.at[px * 2 + pc], r1.at[xc], dev(px, y, z, pc))
 
@@ -258,7 +258,7 @@
     arrived(G_P1, r1.at[pl.ds(0, 7)])
     for k in range(8):
         t1[k] = r1[:, k, :]
-    for k in range(1, 8):
+    for k in (4, 3, 5, 2, 6, 1, 7):
         pz = lax.rem(z + k, NZ_)
         start(G_P2, t1.at[pz], r2.at[z], dev(x, y, pz, c))
     r2[z] = t1[z]
@@ -304,11 +304,11 @@
     def first(q, carry):
         cols = pl.ds(pl.multiple_of(q * BLK, BLK), BLK)
         pre = tn(feats16, w_in16[:, cols].astype(BF16)) + b_in[:, cols]
-        sig = jax.nn.sigmoid(pre)
+        sig = 0.5 * jnp.tanh(0.5 * pre) + 0.5
         hidden = pre * sig
         h1t[:, cols] = hidden.astype(BF16)
         ds1[:, cols] = sig * (1.0 + pre * (1.0 - sig))
-        h1[cols, :] = hidden.T.astype(BF16)
+        h1[cols, :] = hidden.astype(BF16).T
         return carry
 
     lax.fori_loop(0, NBLK, first, 0)
@@ -326,9 +326,9 @@
         return dev(x + k * p, y + k * (1 - p), z, c)
 
     def s1(q):
-        arrived(B_CORE + q, cb.at[q])
-        for p in range(2):
-            a1[q, p] = a1[q, p] + cb[q, :, 128 * p : 128 * p + 128]
+        for p in range(2):
+            arrived(B_CORE + 2 * q + p, cb.at[q, p])
+            a1[q, p] = a1[q, p] + cb[q, p]
             for k in (2, 1, 3):
                 to = lax.rem(me1(p) + k, 4)
                 rows = pl.ds(pl.multiple_of(to * 128, 128), 128)
@@ -339,13 +339,15 @@
     def second(q, carry):
         cols = pl.ds(pl.multiple_of(q * BLK, BLK), BLK)
         pre = nn(h1t[...], w_mid[:, cols]) + b_mid[:, cols]
-        sig = jax.nn.sigmoid(pre)
+        sig = 0.5 * jnp.tanh(0.5 * pre) + 0.5
         hidden = (pre * sig).astype(BF16)
         h2t[:, cols] = hidden
         delta = (back2[:, cols] * (sig * (1.0 + pre * (1.0 - sig)))).astype(BF16)
         g2t[:, cols] = delta
-        cs[q] = nn(h1[pl.ds(pl.multiple_of((1 - c) * half, half), half), :], delta)
-        start(B_CORE + q, cs.at[q], cb.at[q], sibling)
+        other = nn(h1[pl.ds(pl.multiple_of((1 - c) * half, half), half), :], delta)
+        for p in range(2):
+            cs[q, p] = other[:, 128 * p : 128 * p + 128]
+            start(B_CORE + 2 * q + p, cs.at[q, p], cb.at[q, p], sibling)
         own = nn(h1[pl.ds(pl.multiple_of(c * half, half), half), :], delta)
         a1[q, 0] = own[:, 0:128]
         a1[q, 1] = own[:, 128:256]
@@ -558,10 +560,10 @@
     left(G_S3, b3.at[0])
     left(G_S5, sb2)
     for q in range(NBLK):
-        left(B_CORE + q, cb.at[q])
         left(B_RZ + q, b3.at[q])
         left(B_GZ + q, b3.at[q])
         for p in range(2):
+            left(B_CORE + 2 * q + p, cb.at[q, p])
             left(B_R1 + 2 * q + p, b1.at[q, p])
             left(B_R2 + 2 * q + p, b2.at[q, p])
             left(B_G2 + 2 * q + p, b2.at[q, p])
@@ -660,8 +662,8 @@
             tiles(CELLS, HID, dtype=BF16),
             tiles(CELLS, HID, dtype=BF16),
             tiles(CELLS, HID, dtype=BF16),
-            tiles(NBLK, HID // 2, BLK),
-            tiles(NBLK, HID // 2, BLK),
+            tiles(NBLK, 2, HID // 2, 128),
+            tiles(NBLK, 2, HID // 2, 128),
             tiles(NBLK, 2, HID // 2, 128),
             tiles(NBLK, 2, 3, 128, 128),
             tiles(NBLK, 2, 128, 128),

time: 70.7 us -> 70.7 us (level)
  no operation moved by 1% of the time
where the time goes in v3:
time: 70.7 us; the launch traced here: 70.6 us
  Pallas kernels  69.3 us (98%)
  between operations  1.3 us (2%)
    pallas_call x1, Pallas kernels, shards(): pl.pallas_call(body, name='adjoint', out_shape=(pltpu.VMEM((HID, HID), F3...  66.5 us
    pallas_call x1, Pallas kernels, shards(): pl.pallas_call(finish, name='finish', out_shape=out, in_specs=[vmem, vmem...  2.73 us

profile of v3, /device:TPU:1, one launch (start us, length us, event | category | flops | bytes accessed | tf_op | source)
XLA Modules:
  0.0 70.6 jit_solution(7776726982172663197)
XLA Ops:
  1.3 66.5 %adjoint.1 = (f32[1024,1024]{1,0:T(8,128)S(1)}, f32[32,1024]{1,0:T(8,128)S(1)}, f32[16,512]{1,0:T(8,128)S(1)}) custom-call(f32[3,2,2,128]{3,2,1,0:T(2,128)} %velocity_in.1, f32[3,512]{1,0:T(4,128)} %slip_in.1, f32[1,512]{1,0:T(1,128)} %bitcast.13, s32[1,512]{1,0:T(1,128)} %bitcast.14, s32[1,512]{1,0:T(1,128)} %bitcast.15, s32[1]{0:T(128)S(6)} %copy.21.cnt, ...), custom_call_target="tpu_custom_call" | custom-call | tf_op jit(solution)/shard_map/adjoint/pallas_call | solution.py:623
  67.8 2.7 %finish.1 = (f32[6,2,2,128]{3,2,1,0:T(2,128)}, f32[3,2,2,128]{3,2,1,0:T(2,128)}, f32[3,512]{1,0:T(4,128)}, f32[1,512]{1,0:T(1,128)}, f32[12,1024]{1,0:T(8,128)},...) custom-call(f32[1024,1024]{1,0:T(8,128)S(1)} %get-tuple-element.21.big, ...), custom_call_target="tpu_custom_call" | custom-call | tf_op jit(solution)/shard_map/finish/pallas_call | solution.py:727
